TPU v7x, 32 devices: a whole 2x2x4 slice. The times are simulated.
32 devices in a mesh: groups: 2 (over y), band: 4 (over z), wave: 2 (over x), probe: 2 (over core).
Axes of the slice: x: 2, y: 2, z: 4, core: 2. Of those that a mesh axis runs over, the one named last changes fastest.
Arguments:
- probes_spec: bfloat16 [8, 8, 2, 640, 1280], P(('groups', 'probe'), None, None, ('band', 'wave')), parts along dimension 0, may hold values from -6 to 6
- legendre: bfloat16 [640, 16, 1280], P(('band', 'wave')), may hold values from -0.15625 to 0.15625
- wave_order: int32 [640], replicated, may hold values from 0 to 639, each once
- obs_weight: float32 [4, 4096], P(None, ('groups', 'band', 'wave')), parts along dimension 1, may hold values from 0.25 to 4
- send_rows: int32 [16, 8, 32], P(('groups', 'band', 'wave')), parts along dimension 0, may hold values from 0 to 255, as said below
- send_counts: int32 [16, 8], P('groups'), parts along dimension 0, may hold values from 8 to 32, as said below
- interp_idx: int32 [4, 16, 8, 32], P(None, ('groups', 'band', 'wave')), parts along dimension 1, may hold values from 0 to 5119, as said below
- interp_weight: float32 [4, 16, 8, 32], P(None, ('groups', 'band', 'wave')), parts along dimension 1, may hold values from 0 to 1, as said below
Outputs:
- product: bfloat16 [8, 8, 2, 640, 1280], P(('groups', 'probe'), None, None, ('band', 'wave')), parts along dimension 0
There are 2 independent parts, one for each index of `groups`. A program takes and returns all parts, laid end to end along the dimension named above; an argument that names none is the same for every part. Nothing has to cross between parts.
Inputs may be any that keep to these rules, and one draw needn't show every extreme that they name: For each source r, the entries of send_rows[r] are a permutation of 0 to 255. `send_counts`: a count of live slots, at least 8; in every draw one band owner receives 32 live slots from every source. `interp_idx`: the four entries of a slot are the points (i, j), (i, j + 1 mod 1280), (i + 1, j), (i + 1, j + 1 mod 1280) of the band owner's rows, as i * 1280 + j. `interp_weight`: the four weights of a slot are nonnegative and sum to 1.
All inputs are finite; a program needn't handle non-finite values.
Results may differ from a plain program's by a relative error of at most 0.0083.
Values may be sent and summed in bfloat16 or wider, within the bound.
A program may use at most 64 MiB of HBM per device.

v0:
```python
import math

import jax
import jax.numpy as jnp
from jax import lax
from jax.sharding import PartitionSpec as P

NLON = 1280


def make_basis(wave_numbers, lon_count, wave_total):
    columns = jnp.arange(lon_count, dtype=jnp.int32)
    phases = wave_numbers[:, None] * columns[None, :] % lon_count
    angles = phases.astype(jnp.float32) * (2.0 * math.pi / lon_count)
    factor = 1.0 / math.sqrt(wave_total)
    return jnp.stack([factor * jnp.cos(angles), -factor * jnp.sin(angles)]).astype(jnp.bfloat16)


def on_device(
    probes_spec, legendre, wave_order, obs_weight, send_rows, send_counts, interp_idx, interp_weight
):
    band_count = lax.axis_size("band")
    wave_count = lax.axis_size("wave")
    node_count = band_count * wave_count
    probe_local, field_count, _, slot_local, degree_count = probes_spec.shape
    field_local = field_count // wave_count
    lat_local = legendre.shape[1] // band_count
    wave_total = wave_order.shape[0]
    capacity = send_rows.shape[2]
    points = lat_local * NLON
    spec_split = probes_spec.reshape(
        probe_local, wave_count, field_local, 2, slot_local, degree_count
    )
    legendre_split = legendre.reshape(slot_local, band_count, lat_local, degree_count)
    fourier = jnp.einsum(
        "pwgksn,sbln->bwpglks", spec_split, legendre_split, preferred_element_type=jnp.float32
    ).astype(jnp.bfloat16)
    fourier_basis = make_basis(wave_order, NLON, wave_total)
    flat_fourier = fourier.reshape(node_count, probe_local, field_local, lat_local, 2, slot_local)
    grid_values = jnp.einsum(
        "pglks,ksj->pglj",
        lax.all_to_all(flat_fourier, ("band", "wave"), split_axis=0, concat_axis=5, tiled=True)[0],
        fourier_basis,
        preferred_element_type=jnp.float32,
    )
    grid_flat = grid_values.reshape(probe_local, field_local, points)
    node_index = lax.axis_index(("band", "wave"))
    counts_here = lax.dynamic_slice_in_dim(send_counts, node_index, 1, 1)[:, 0]
    live_mask = jnp.arange(capacity, dtype=jnp.int32)[None, :] < counts_here[:, None]
    corner_index = interp_idx[:, 0].reshape(-1)
    corner_weight = interp_weight[:, 0]
    values = jnp.take(grid_flat, corner_index, axis=2).reshape(
        probe_local, field_local, 4, node_count, capacity
    )
    corner_sums = jnp.sum(values * corner_weight[None, None], axis=2)
    observed = jnp.where(live_mask[None, None], corner_sums, 0.0).astype(jnp.bfloat16)
    record_index = send_rows[0].reshape(-1)
    slot_weight = jnp.take(obs_weight, record_index, axis=1).reshape(
        field_local, node_count, capacity
    )
    scaled = (
        slot_weight[None]
        * lax.all_to_all(
            observed, ("band", "wave"), split_axis=2, concat_axis=2, tiled=True
        ).astype(jnp.float32)
    ).astype(jnp.bfloat16)
    weighted = lax.all_to_all(scaled, ("band", "wave"), split_axis=2, concat_axis=2, tiled=True)
    scattered = (corner_weight[None, None] * weighted.astype(jnp.float32)[:, :, None]).reshape(
        probe_local, field_local, -1
    )
    adjoint = (
        jnp.zeros((probe_local, field_local, points), jnp.float32)
        .at[:, :, corner_index]
        .add(scattered)
    )
    adjoint = adjoint.reshape(probe_local, field_local, lat_local, NLON).astype(jnp.bfloat16)
    fourier_adjoint = jnp.einsum(
        "pglj,ksj->pglks", adjoint, fourier_basis, preferred_element_type=jnp.float32
    ).astype(jnp.bfloat16)
    split_adjoint = fourier_adjoint.reshape(
        probe_local, field_local, lat_local, 2, node_count, slot_local
    )
    received = lax.all_to_all(
        split_adjoint, ("band", "wave"), split_axis=4, concat_axis=4, tiled=True
    )
    item_count = received.shape[0]
    parted = received.reshape(
        item_count, field_local, lat_local, 2, band_count, wave_count, slot_local
    )
    result = jnp.einsum(
        "pglkbws,sbln->pwgksn", parted, legendre_split, preferred_element_type=jnp.float32
    )
    return result.reshape(item_count, field_count, 2, slot_local, degree_count).astype(jnp.bfloat16)


def solution(mesh):
    placed = (
        P(("groups", "probe"), None, None, ("band", "wave"), None),
        P(("band", "wave"), None, None),
        P(),
        P(None, ("groups", "band", "wave")),
        P(("groups", "band", "wave"), None, None),
        P("groups", None),
        P(None, ("groups", "band", "wave"), None, None),
        P(None, ("groups", "band", "wave"), None, None),
    )
    return jax.shard_map(
        on_device,
        mesh=mesh,
        in_specs=placed,
        out_specs=P(("groups", "probe"), None, None, ("band", "wave"), None),
        check_vma=False,
    )
```

profile of v0, /device:TPU:0, one launch (start us, length us, event | category | flops | bytes accessed | tf_op | source)
XLA Modules:
  0.0 306.2 jit_solution(2593126921165463928)
XLA Ops:
  0.0 5.4 %reshape.246 = bf16[80,4,4,1280,1,1,1]{3,2,1,0,4,5,6:T(4,128)(2,1)S(1)} reshape(bf16[80,16,1280]{2,1,0:T(8,128)(2,1)} %param.9) | data formatting | bytes 6553600 | tf_op jit(solution)/shard_map/reshape | solution.py:34
  5.4 66.7 %convert_bitcast_fusion = bf16[4,2,2,4,4,2,80]{3,4,5,1,2,0,6:T(4,128)(2,1)} fusion(bf16[2,2,4,2,80,1280,1]{5,4,3,2,1,0,6:T(8,128)(2,1)} %bitcast.96, bf16[80,4,4,1280,1,1,1]{3,2,1,0,4,5,6:T(4,128)(2,1)S(1)} %reshape.246), kind=kOutput, calls=%fused_computation.19 | convolution fusion | flops 104898560 | bytes 9912320 | tf_op jit(solution)/shard_map/pwgksn,sbln->bwpglks/dot_general | solution.py:35
  72.1 4.6 %copy.52 = bf16[4,2,2,4,4,2,80]{6,1,0,5,4,3,2:T(2,128)(2,1)S(1)} copy(bf16[4,2,2,4,4,2,80]{3,4,5,1,2,0,6:T(4,128)(2,1)} %convert_bitcast_fusion) | data formatting | bytes 163840 | tf_op jit(solution)/shard_map/convert_element_type | solution.py:37
  76.7 0.8 copy.53
  77.5 7.3 %all-to-all-start = ((bf16[8,2,4,4,2,80]{5,4,3,2,1,0:T(2,128)(2,1)}), bf16[8,2,4,4,2,80]{5,4,3,2,1,0:T(2,128)(2,1)S(1)}, u32[]{:S(2)}, u32[]{:S(2)}) async-start(bf16[8,2,4,4,2,80]{5,4,3,2,1,0:T(2,128)(2,1)} %copy.53), calls=%async_computation | async-start | bytes 262144 | tf_op jit(solution)/shard_map/all_to_all | solution.py:42
  86.1 0.8 copy.49
  86.9 15.9 %multiply_convert_fusion.1 = (bf16[1,640,1280]{2,1,0:T(8,128)(2,1)S(1)}, bf16[1,640,1280]{2,1,0:T(8,128)(2,1)S(1)}) fusion(s32[640]{0:T(1024)} %param.10), kind=kLoop, calls=%fused_computation.14 | loop fusion | flops 10649600 | bytes 3279360 | tf_op jit(solution)/shard_map/convert
  102.9 0.9 dynamic-slice_reduce_fusion
  103.8 1.5 gather_fusion
  105.3 1.3 iota_compare_fusion
  106.6 0.8 squeeze.3
  107.4 1.6 convolution_bitcast_fusion
  109.1 5.4 %copy.73 = f32[2,4,4,1280]{1,0,3,2:T(2,128)} copy(f32[2,4,4,1280]{3,2,1,0:T(4,128)S(1)} %convolution_bitcast_fusion) | data formatting | bytes 327680 | tf_op jit(solution)/shard_map/reshape | solution.py:46
  114.4 6.0 %gather_fusion.1 = f32[1024,2,4]{2,1,0:T(2,128)S(1)} fusion(f32[2,4,5120]{1,0,2:T(2,128)} %bitcast.83, s32[1024]{0:T(1024)S(1)} %broadcast_clamp_fusion), kind=kCustom, calls=%fused_computation.1 | custom fusion | bytes 69632 | tf_op jit(solution)/shard_map/jit(_take)/gather | solution.py:52
  120.5 3.0 multiply_reduce_fusion
  124.0 0.7 reshape.254
  124.7 6.0 %all-to-all-start.1 = ((bf16[8,2,128]{2,1,0:T(2,128)(2,1)}), bf16[8,2,128]{2,1,0:T(2,128)(2,1)S(1)}, u32[]{:S(2)}, u32[]{:S(2)}) async-start(bf16[8,2,128]{2,1,0:T(2,128)(2,1)} %reshape.254), calls=%async_computation.1 | async-start | bytes 8192 | tf_op jit(solution)/shard_map/all_to_all | solution.py:63
  130.7 1.0 broadcast_select_fusion.1
  131.8 5.3 %all-to-all-done.1 = bf16[8,2,128]{2,1,0:T(2,128)(2,1)S(1)} async-done(((bf16[8,2,128]{2,1,0:T(2,128)(2,1)}), bf16[8,2,128]{2,1,0:T(2,128)(2,1)S(1)}, u32[]{:S(2)}, u32[]{:S(2)}) %all-to-all-start.1) | async-done | bytes 4128 | tf_op jit(solution)/shard_map/all_to_all | solution.py:63
  137.2 0.7 reshape.256
  137.9 3.3 %all-to-all-start.2 = ((bf16[8,2,128]{2,1,0:T(2,128)(2,1)}), bf16[8,2,128]{2,1,0:T(2,128)(2,1)S(1)}, u32[]{:S(2)}, u32[]{:S(2)}) async-start(bf16[8,2,128]{2,1,0:T(2,128)(2,1)} %reshape.256), calls=%async_computation.2 | async-start | bytes 8192 | tf_op jit(solution)/shard_map/all_to_all | solution.py:67
  141.2 6.3 %all-to-all-done.2 = bf16[8,2,128]{2,1,0:T(2,128)(2,1)S(1)} async-done(((bf16[8,2,128]{2,1,0:T(2,128)(2,1)}), bf16[8,2,128]{2,1,0:T(2,128)(2,1)S(1)}, u32[]{:S(2)}, u32[]{:S(2)}) %all-to-all-start.2) | async-done | bytes 4128 | tf_op jit(solution)/shard_map/all_to_all | solution.py:67
  147.8 2.9 bitcast_multiply_fusion
  150.7 3.7 %broadcast_in_dim.41 = f32[2,4,5120]{1,0,2:T(2,128)} broadcast(f32[]{:T(128)} %constant.31.clone.1), dimensions={} | broadcast | bytes 163844 | tf_op jit(solution)/shard_map/broadcast_in_dim | solution.py:72
  154.4 102.8 %scatter_fusion = f32[2,4,5120]{1,0,2:T(2,128)} fusion(f32[2,4,5120]{1,0,2:T(2,128)} %broadcast_in_dim.41, s32[1024]{0:T(1024)S(1)} %bitcast.94, f32[1024,2,4]{2,1,0:T(2,128)S(1)} %bitcast.84), kind=kCustom, calls=%fused_computation.2 | custom fusion | flops 8192 | bytes 102400 | tf_op jit(solution)/shard_map/scatter-add | solution.py:74
  257.2 4.8 %convert_element_type.58 = bf16[2,4,5120]{1,0,2:T(2,128)(2,1)S(1)} convert(f32[2,4,5120]{1,0,2:T(2,128)} %scatter_fusion) | non-fusion elementwise | flops 40960 | bytes 245760 | tf_op jit(solution)/shard_map/convert_element_type | solution.py:76
  262.0 1.9 copy.68
  263.9 3.2 %fusion.15 = bf16[2,4,4,2,640]{4,2,3,1,0:T(4,128)(2,1)S(1)} fusion(bf16[2,4,4,1280,1]{3,2,4,1,0:T(4,128)(2,1)S(1)} %copy.68, bf16[1,640,1280]{2,1,0:T(8,128)(2,1)} %copy-done.4, bf16[1,640,1280]{2,1,0:T(8,128)(2,1)} %copy-done.3), kind=kOutput, calls=%fused_computation.22 | convolution fusion | flops 111452160 | bytes 3440640 | tf_op jit(solution)/shard_map/pglj,ksj->pglks/dot_general | solution.py:77
  267.4 9.9 %all_to_all.30 = bf16[2,4,4,2,8,80]{5,3,2,1,0,4:T(2,128)(2,1)S(1)} all-to-all(bf16[2,4,4,2,8,80]{5,3,2,1,0,4:T(2,128)(2,1)S(1)} %copy.60), channel_id=1, replica_groups=mesh['groups'=2,'band'=4,'wave'=2,'probe'=2] {'band','wave'}, dimensions={4} | all-to-all | bytes 163840 | tf_op jit(solution)/shard_map/all_to_all | solution.py:83
  277.4 4.6 %copy.62 = bf16[2,4,4,2,4,2,80]{2,1,4,5,3,0,6:T(4,128)(2,1)} copy(bf16[2,4,4,2,4,2,80]{6,3,2,1,0,5,4:T(2,128)(2,1)S(1)} %bitcast.88) | data formatting | bytes 163840 | tf_op jit(solution)/shard_map/reshape | solution.py:87
  282.0 14.6 %fusion = bf16[2,2,4,2,80,1280]{5,2,1,3,0,4:T(4,128)(2,1)} fusion(bf16[2,4,4,2,4,2,80]{2,1,4,5,3,0,6:T(4,128)(2,1)} %copy.62, bf16[80,4,4,1280,1,1,1]{3,2,1,0,4,5,6:T(4,128)(2,1)S(1)} %copy-done.2), kind=kOutput, calls=%fused_computation.4 | convolution fusion | flops 108134400 | bytes 9912320 | tf_op jit(solution)/shard_map/pglkbws,sbln->pwgksn/dot_general | solution.py:90
  296.6 9.3 %copy.78 = bf16[2,2,4,2,80,1280]{5,4,3,2,1,0:T(8,128)(2,1)} copy(bf16[2,2,4,2,80,1280]{5,2,1,3,0,4:T(4,128)(2,1)} %fusion) | data formatting | bytes 13107200 | tf_op jit(solution)/shard_map/convert_element_type | solution.py:93
  (41 shorter events, 2.8 us)
Async XLA Ops:
  0.0 102.9 %copy-start = (s32[8,8]{1,0:T(8,128)S(1)}, s32[8,8]{1,0:T(8,128)}, u32[]{:S(2)}) copy-start(s32[8,8]{1,0:T(8,128)} %param.13) | copy-start | bytes 772
  5.4 66.7 %copy-start.1 = (bf16[80,4,4,1280,1,1,1]{3,2,1,0,4,5,6:T(4,128)(2,1)}, bf16[80,4,4,1280,1,1,1]{3,2,1,0,4,5,6:T(4,128)(2,1)S(1)}, u32[]{:S(2)}) copy-start(bf16[80,4,4,1280,1,1,1]{3,2,1,0,4,5,6:T(4,128)(2,1)S(1)} %reshape.246) | copy-start | bytes 9830404
  72.1 12.6 %copy-start.7 = (s32[1,8,32]{2,1,0:T(8,128)S(1)}, s32[1,8,32]{2,1,0:T(8,128)}, u32[]{:S(2)}) copy-start(s32[1,8,32]{2,1,0:T(8,128)} %param.12) | copy-start | bytes 3076
  72.1 13.3 %copy-start.6 = (s32[4,1,8,32]{3,2,1,0:T(8,128)S(1)}, s32[4,1,8,32]{3,2,1,0:T(8,128)}, u32[]{:S(2)}) copy-start(s32[4,1,8,32]{3,2,1,0:T(8,128)} %param.14) | copy-start | bytes 12292
  77.5 29.0 %all-to-all-start = ((bf16[8,2,4,4,2,80]{5,4,3,2,1,0:T(2,128)(2,1)}), bf16[8,2,4,4,2,80]{5,4,3,2,1,0:T(2,128)(2,1)S(1)}, u32[]{:S(2)}, u32[]{:S(2)}) async-start(bf16[8,2,4,4,2,80]{5,4,3,2,1,0:T(2,128)(2,1)} %copy.53), calls=%async_computation | async-start | bytes 262144 | tf_op jit(solution)/shard_map/all_to_all | solution.py:42
  102.9 6.2 %copy-start.3 = (bf16[1,640,1280]{2,1,0:T(8,128)(2,1)}, bf16[1,640,1280]{2,1,0:T(8,128)(2,1)S(1)}, u32[]{:S(2)}) copy-start(bf16[1,640,1280]{2,1,0:T(8,128)(2,1)S(1)} %get-tuple-element.5) | copy-start | bytes 4915204
  102.9 6.2 %copy-start.4 = (bf16[1,640,1280]{2,1,0:T(8,128)(2,1)}, bf16[1,640,1280]{2,1,0:T(8,128)(2,1)S(1)}, u32[]{:S(2)}) copy-start(bf16[1,640,1280]{2,1,0:T(8,128)(2,1)S(1)} %get-tuple-element.6) | copy-start | bytes 4915204
  109.0 11.4 %copy-start.5 = (f32[4,1,8,32]{3,2,1,0:T(8,128)S(1)}, f32[4,1,8,32]{3,2,1,0:T(8,128)}, u32[]{:S(2)}) copy-start(f32[4,1,8,32]{3,2,1,0:T(8,128)} %param.15) | copy-start | bytes 12292
  109.1 14.4 %copy-start.9 = (pred[8,32]{1,0:T(8,128)(4,1)S(1)}, pred[8,32]{1,0:T(8,128)(4,1)}, u32[]{:S(2)}) copy-start(pred[8,32]{1,0:T(8,128)(4,1)} %iota_compare_fusion) | copy-start | bytes 772
  109.1 21.6 %copy-start.8 = (pred[8,32]{1,0:T(8,128)(4,1)S(1)}, pred[8,32]{1,0:T(8,128)(4,1)}, u32[]{:S(2)}) copy-start(pred[8,32]{1,0:T(8,128)(4,1)} %compare_and_fusion.1) | copy-start | bytes 772
  124.7 12.4 %all-to-all-start.1 = ((bf16[8,2,128]{2,1,0:T(2,128)(2,1)}), bf16[8,2,128]{2,1,0:T(2,128)(2,1)S(1)}, u32[]{:S(2)}, u32[]{:S(2)}) async-start(bf16[8,2,128]{2,1,0:T(2,128)(2,1)} %reshape.254), calls=%async_computation.1 | async-start | bytes 8192 | tf_op jit(solution)/shard_map/all_to_all | solution.py:63
  137.9 9.6 %all-to-all-start.2 = ((bf16[8,2,128]{2,1,0:T(2,128)(2,1)}), bf16[8,2,128]{2,1,0:T(2,128)(2,1)S(1)}, u32[]{:S(2)}, u32[]{:S(2)}) async-start(bf16[8,2,128]{2,1,0:T(2,128)(2,1)} %reshape.256), calls=%async_computation.2 | async-start | bytes 8192 | tf_op jit(solution)/shard_map/all_to_all | solution.py:67
  263.9 18.1 %copy-start.2 = (bf16[80,4,4,1280,1,1,1]{3,2,1,0,4,5,6:T(4,128)(2,1)S(1)}, bf16[80,4,4,1280,1,1,1]{3,2,1,0,4,5,6:T(4,128)(2,1)}, u32[]{:S(2)}) copy-start(bf16[80,4,4,1280,1,1,1]{3,2,1,0,4,5,6:T(4,128)(2,1)} %copy-done.1) | copy-start | bytes 9830404
where the time goes:
time: 309 us; the launch traced here: 306 us
  other arithmetic  133 us (43%)
  matrix products  86.1 us (28%)
  local copies, waits for them, and re-layouts  48.3 us (16%)
  starting transfers between devices  16.6 us (5%)
  waiting for transfers between devices  11.5 us (4%)
  blocking collectives  9.94 us (3%)
    scatter-add x1, other arithmetic, on_device(): adjoint = jnp.zeros((probe_local, field_local, points), jnp.float32).at[:...  103 us
    dot_general x1, matrix products, on_device(): jnp.einsum('pwgksn,sbln->bwpglks', spec_split, legendre_split, preferred_...  66.7 us
    another operation x1, other arithmetic  15.9 us
    dot_general x1, matrix products, on_device(): jnp.einsum('pglkbws,sbln->pwgksn', parted, legendre_split, preferred_elem...  14.6 us
    all_to_all x1, blocking collectives, on_device(): lax.all_to_all(split_adjoint, ('band', 'wave'), split_axis=4, concat_axis...  9.94 us
    convert_element_type x1, local copies, waits for them, and re-layouts, on_device(): result.reshape(item_count, field_count, 2, slot_local, degree_count)  9.27 us
    all_to_all x1, starting transfers between devices, on_device(): lax.all_to_all(flat_fourier, ('band', 'wave'), split_axis=0, concat_axis=...  7.25 us
    all_to_all x1, waiting for transfers between devices, on_device(): lax.all_to_all(scaled, ('band', 'wave'), split_axis=2, concat_axis=2, til...  6.25 us
  transfers between devices with their start and end apart: 3, of which 2 were waited for; matrix products, arithmetic and copies ran while one was open for 7% of the time, Pallas kernels for 0%

commit v1 on v0

--- a/solution.py
+++ b/solution.py
@@ -1,11 +1,359 @@
+import functools
 import math
 
 import jax
 import jax.numpy as jnp
 from jax import lax
+from jax.experimental import pallas as pl
+from jax.experimental.pallas import tpu as pltpu
 from jax.sharding import PartitionSpec as P
 
 NLON = 1280
+SB = 16
+F32 = jnp.float32
+BF16 = jnp.bfloat16
+NT = (((1,), (1,)), ((), ()))
+TN = (((0,), (0,)), ((), ()))
+
+
+def dot(a, b, dims=(((1,), (0,)), ((), ()))):
+    return lax.dot_general(a, b, dims, preferred_element_type=F32)
+
+
+def iota(shape, dim):
+    return lax.broadcasted_iota(jnp.int32, shape, dim)
+
+
+def cos_sin(phase):
+    quarter = jnp.floor(phase * (4.0 / NLON) + 0.5)
+    x = (phase - quarter * (NLON // 4)) * (2.0 * math.pi / NLON)
+    x2 = x * x
+    s = x * (1.0 + x2 * (-1 / 6 + x2 * (1 / 120 + x2 * (-1 / 5040 + x2 * (1 / 362880)))))
+    c = 1.0 + x2 * (-0.5 + x2 * (1 / 24 + x2 * (-1 / 720 + x2 * (1 / 40320))))
+    turn = quarter - 4.0 * jnp.floor(quarter * 0.25)
+    odd = (turn == 1.0) | (turn == 3.0)
+    cos = jnp.where(odd, s, c) * jnp.where((turn == 1.0) | (turn == 2.0), -1.0, 1.0)
+    sin = jnp.where(odd, c, s) * jnp.where(turn >= 2.0, -1.0, 1.0)
+    return cos, sin
+
+
+def selector(lat, items):
+    shape = (lat * items, items * SB * lat)
+    row, col = iota(shape, 0), iota(shape, 1)
+    same = (row // items == col % lat) & (row % items == col // (SB * lat))
+    return jnp.where(same, 1.0, 0.0).astype(BF16)
+
+
+def exchange_kernel(
+    bands, waves, probes_hbm, legendre_hbm, wave_ref, obs_ref, rows_ref, counts_ref, idx_ref,
+    weight_ref, out_ref, probe_buf, leg_buf, spread, basis, corner, send_w, recv_w, slot_w,
+    send_1, recv_1, send_2, recv_2, lanes, point, weights, probe_sem, leg_sem, tx_w, rx_w, tx_1,
+    rx_1, tx_2, rx_2,
+):
+    nodes = bands * waves
+    _, probe_local, field_count, _, _, degrees = probe_buf.shape
+    blocks, _, lat, _ = leg_buf.shape
+    slots = blocks * SB
+    fields = field_count // waves
+    items = probe_local * fields
+    lat_local = lat // bands
+    rows = lat_local * items
+    capacity = rows_ref.shape[2]
+    total = nodes * slots
+    band, wave = lax.axis_index("band"), lax.axis_index("wave")
+    me = band * waves + wave
+
+    def where_is(node):
+        return {"band": node // waves, "wave": node % waves}
+
+    def peer(step):
+        return lax.rem(me + step, nodes)
+
+    def copies(send, recv, tx, rx):
+        return [
+            pltpu.make_async_remote_copy(
+                src_ref=send.at[peer(step)],
+                dst_ref=recv.at[me],
+                send_sem=tx.at[step],
+                recv_sem=rx.at[step],
+                device_id=where_is(peer(step)),
+                device_id_type=pl.DeviceIdType.MESH,
+            )
+            for step in range(1, nodes)
+        ]
+
+    def load(block):
+        part = pl.ds(block * SB, SB)
+        return (
+            pltpu.make_async_copy(
+                probes_hbm.at[:, :, :, part, :], probe_buf.at[block], probe_sem.at[block]
+            ),
+            pltpu.make_async_copy(legendre_hbm.at[part], leg_buf.at[block], leg_sem.at[block]),
+        )
+
+    for block in range(blocks):
+        for one in load(block):
+            one.start()
+    barrier = pltpu.get_barrier_semaphore()
+    for step in range(1, nodes):
+        pl.semaphore_signal(
+            barrier, inc=1, device_id=where_is(peer(step)), device_id_type=pl.DeviceIdType.MESH
+        )
+
+    obs = jnp.concatenate([obs_ref[...]] * probe_local, axis=0)
+    high = obs.astype(BF16).astype(F32)
+    middle = (obs - high).astype(BF16).astype(F32)
+    split = jnp.concatenate([high, middle, obs - high - middle], axis=0).astype(BF16)
+    record = rows_ref[0]
+    for node in range(nodes):
+        pick = iota((obs.shape[1], capacity), 0) == record[node : node + 1, :]
+        found = dot(split, jnp.where(pick, 1.0, 0.0).astype(BF16))
+        send_w[node] = found[2 * items :] + found[items : 2 * items] + found[:items]
+    pl.semaphore_wait(barrier, nodes - 1)
+    copies_w = copies(send_w, recv_w, tx_w, rx_w)
+    for one in copies_w:
+        one.start()
+    recv_w[me] = send_w[me]
+
+    counts = counts_ref[...].astype(F32)
+    mine = jnp.sum(jnp.where(iota(counts.shape, 1) == me, counts, 0.0), axis=1, keepdims=True)
+    live = iota((nodes, capacity), 1).astype(F32) < mine
+    for i in range(4):
+        live_weight = jnp.where(live, weight_ref[i, 0], 0.0)
+        for node in range(nodes):
+            at = slice(node * capacity, (node + 1) * capacity)
+            weights[i : i + 1, at] = live_weight[node : node + 1]
+    for i in range(2):
+        for node in range(nodes):
+            at = slice(node * capacity, (node + 1) * capacity)
+            point[i : i + 1, at] = idx_ref[i, 0, node : node + 1, :].astype(F32)
+
+    choose = selector(lat, items)
+
+    @pl.loop(0, blocks)
+    def _(block):
+        for one in load(block):
+            one.wait()
+        product = dot(
+            probe_buf[block].reshape(probe_local * field_count * 2 * SB, degrees),
+            leg_buf[block].reshape(SB * lat, degrees),
+            NT,
+        )
+        own = iota(product.shape, 0) % SB == iota(product.shape, 1) // lat
+        product = jnp.where(own, product, 0.0).astype(BF16)
+        for p in range(probe_local):
+            for w in range(waves):
+                for e in range(fields):
+                    for k in range(2):
+                        first = (((p * waves + w) * fields + e) * 2 + k) * SB
+                        item = (p * fields + e) * SB * lat
+                        spread[w, k, block, :, item : item + SB * lat] = product[first : first + SB]
+
+    for w in range(waves):
+        fourier = dot(choose, spread[w].reshape(2 * slots, items * SB * lat), NT).astype(BF16)
+        for b in range(bands):
+            send_1[b * waves + w] = fourier[b * rows : (b + 1) * rows]
+    copies_1 = copies(send_1, recv_1, tx_1, rx_1)
+    for one in copies_1:
+        one.start()
+    recv_1[me] = send_1[me]
+
+    factor = 1.0 / math.sqrt(total)
+    for lane in range(0, total, 128):
+        order = wave_ref[:, lane : lane + 128].astype(F32)
+        turn_c, turn_s = cos_sin(order * 128.0)
+
+        @pl.loop(0, 2)
+        def _(half):
+            j = (iota((64, 128), 0) + half * 64).astype(F32)
+            cos, sin = cos_sin(j * order)
+            cos, sin = cos * factor, sin * factor
+            for turn in range(NLON // 128):
+                at = pl.ds(pl.multiple_of(half * 64, 64), 64)
+                basis[turn, at, lane : lane + 128] = cos.astype(BF16)
+                basis[turn, at, total + lane : total + lane + 128] = (-sin).astype(BF16)
+                cos, sin = cos * turn_c - sin * turn_s, sin * turn_c + cos * turn_s
+
+    row_of = jnp.floor((point[0:1, :] + 0.5) * (1.0 / NLON))
+    west = point[0:1, :] - row_of * NLON
+    east = point[1:2, :] - row_of * NLON
+    west_weight, east_weight = [], []
+    for l in range(lat_local):
+        south, north = row_of == float(l), row_of == float(l - 1)
+        west_weight.append(
+            jnp.where(south, weights[0:1, :], jnp.where(north, weights[2:3, :], 0.0))
+        )
+        east_weight.append(
+            jnp.where(south, weights[1:2, :], jnp.where(north, weights[3:4, :], 0.0))
+        )
+
+    @pl.loop(0, NLON // 64)
+    def _(part):
+        j = (iota((64, west.shape[1]), 0) + part * 64).astype(F32)
+        at_west, at_east = j == west, j == east
+        for l in range(lat_local):
+            corner[l, part] = jnp.where(
+                at_west, west_weight[l], jnp.where(at_east, east_weight[l], 0.0)
+            ).astype(BF16)
+
+    for one in copies_w:
+        one.wait()
+    for node in range(nodes):
+        slot_w[:, node * capacity : (node + 1) * capacity] = recv_w[node]
+    for one in copies_1:
+        one.wait()
+    for node in range(nodes):
+        got = recv_1[node].astype(F32)
+        for k in range(2):
+            at = k * total + node * slots
+            lanes[:, at : at + slots] = got[:, k * slots : (k + 1) * slots]
+    table = basis[...].reshape(NLON, 2 * total)
+    grid_values = dot(lanes[...].astype(BF16), table, NT)
+    observed = jnp.zeros((2 * items, nodes * capacity), F32)
+    for l in range(lat_local):
+        here = grid_values[l * items : (l + 1) * items]
+        both = jnp.concatenate([here, here - here.astype(BF16).astype(F32)], axis=0)
+        observed += dot(both.astype(BF16), corner[l].reshape(NLON, nodes * capacity))
+    observed = (observed[:items] + observed[items:]).astype(BF16).astype(F32)
+    weighted = (slot_w[...] * observed).astype(BF16)
+    adjoint = jnp.concatenate(
+        [dot(weighted, corner[l].reshape(NLON, nodes * capacity), NT) for l in range(lat_local)],
+        axis=0,
+    ).astype(BF16)
+    lanes[...] = dot(adjoint, table)
+    for node in range(nodes):
+        at = node * slots
+        send_2[node] = jnp.concatenate(
+            [lanes[:, at : at + slots], lanes[:, total + at : total + at + slots]], axis=1
+        ).astype(BF16)
+    copies_2 = copies(send_2, recv_2, tx_2, rx_2)
+    for one in copies_2:
+        one.start()
+    recv_2[me] = send_2[me]
+    for one in copies_2:
+        one.wait()
+    for b in range(bands):
+        for w in range(waves):
+            out_ref[w, b * rows : (b + 1) * rows, :] = recv_2[b * waves + w]
+
+
+def synthesis_kernel(adjoint_ref, legendre_ref, out_ref, spread):
+    probe_local, field_count, _, _, degrees = out_ref.shape
+    waves = adjoint_ref.shape[0]
+    fields = field_count // waves
+    items = probe_local * fields
+    lat = legendre_ref.shape[1]
+    block = pl.program_id(0)
+
+    @pl.when(block == 0)
+    def _():
+        choose = selector(lat, items)
+        for w in range(waves):
+            wide = dot(adjoint_ref[w], choose, TN)
+            own = iota(wide.shape, 0) % SB == iota(wide.shape, 1) % (SB * lat) // lat
+            spread[w] = jnp.where(own, wide, 0.0).astype(BF16).reshape(spread.shape[1:])
+
+    pieces = []
+    for p in range(probe_local):
+        for w in range(waves):
+            for e in range(fields):
+                for k in range(2):
+                    item = (p * fields + e) * SB * lat
+                    pieces.append(spread[w, k, block, :, item : item + SB * lat])
+    result = dot(
+        jnp.concatenate(pieces, axis=0), legendre_ref[...].reshape(SB * lat, degrees)
+    )
+    out_ref[...] = result.astype(BF16).reshape(out_ref.shape)
+
+
+def fits_kernels(probes_spec, legendre, wave_order, obs_weight, send_rows, bands, waves):
+    probe_local, field_count, _, slots, degrees = probes_spec.shape
+    lat = legendre.shape[1]
+    items = probe_local * field_count // waves
+    return (
+        slots % SB == 0
+        and lat == 16
+        and degrees % 128 == 0
+        and wave_order.shape[0] % 128 == 0
+        and field_count % waves == 0
+        and obs_weight.shape[0] * probe_local == items
+        and items == 8
+        and lat % bands == 0
+        and lat // bands * items % 16 == 0
+        and 1 < bands * waves <= 8
+        and bands * waves * send_rows.shape[2] % 128 == 0
+        and obs_weight.shape[1] <= 1024
+    )
+
+
+def in_kernels(
+    probes_spec, legendre, wave_order, obs_weight, send_rows, send_counts, interp_idx, interp_weight
+):
+    bands = lax.axis_size("band")
+    waves = lax.axis_size("wave")
+    nodes = bands * waves
+    probe_local, field_count, _, slots, degrees = probes_spec.shape
+    lat = legendre.shape[1]
+    blocks = slots // SB
+    items = probe_local * field_count // waves
+    rows = lat // bands * items
+    total = wave_order.shape[0]
+    capacity = send_rows.shape[2]
+    wide = items * SB * lat
+    vmem = pl.BlockSpec(memory_space=pltpu.VMEM)
+    hbm = pl.BlockSpec(memory_space=pl.ANY)
+    dma = pltpu.SemaphoreType.DMA
+    adjoint = pl.pallas_call(
+        functools.partial(exchange_kernel, bands, waves),
+        out_shape=jax.ShapeDtypeStruct((waves, bands * rows, 2 * slots), BF16),
+        in_specs=[hbm, hbm] + [vmem] * 6,
+        out_specs=vmem,
+        scratch_shapes=[
+            pltpu.VMEM((blocks, probe_local, field_count, 2, SB, degrees), BF16),
+            pltpu.VMEM((blocks, SB, lat, degrees), BF16),
+            pltpu.VMEM((waves, 2, blocks, SB, wide), BF16),
+            pltpu.VMEM((NLON // 128, 128, 2 * total), BF16),
+            pltpu.VMEM((lat // bands, NLON // 64, 64, nodes * capacity), BF16),
+            pltpu.VMEM((nodes, items, capacity), F32),
+            pltpu.VMEM((nodes, items, capacity), F32),
+            pltpu.VMEM((items, nodes * capacity), F32),
+            pltpu.VMEM((nodes, rows, 2 * slots), BF16),
+            pltpu.VMEM((nodes, rows, 2 * slots), BF16),
+            pltpu.VMEM((nodes, rows, 2 * slots), BF16),
+            pltpu.VMEM((nodes, rows, 2 * slots), BF16),
+            pltpu.VMEM((rows, 2 * total), F32),
+            pltpu.VMEM((8, nodes * capacity), F32),
+            pltpu.VMEM((8, nodes * capacity), F32),
+            dma((blocks,)),
+            dma((blocks,)),
+            dma((nodes,)),
+            dma((nodes,)),
+            dma((nodes,)),
+            dma((nodes,)),
+            dma((nodes,)),
+            dma((nodes,)),
+        ],
+        compiler_params=pltpu.CompilerParams(
+            collective_id=0, has_side_effects=True, vmem_limit_bytes=48 * 2**20
+        ),
+    )(
+        probes_spec, legendre, wave_order.reshape(1, total), obs_weight, send_rows, send_counts,
+        interp_idx, interp_weight,
+    )
+    return pl.pallas_call(
+        synthesis_kernel,
+        grid=(blocks,),
+        out_shape=jax.ShapeDtypeStruct(probes_spec.shape, BF16),
+        in_specs=[
+            pl.BlockSpec(adjoint.shape, lambda i: (0, 0, 0)),
+            pl.BlockSpec((SB, lat, degrees), lambda i: (i, 0, 0)),
+        ],
+        out_specs=pl.BlockSpec(
+            (probe_local, field_count, 2, SB, degrees), lambda i: (0, 0, 0, i, 0)
+        ),
+        scratch_shapes=[pltpu.VMEM((waves, 2, blocks, SB, wide), BF16)],
+        compiler_params=pltpu.CompilerParams(vmem_limit_bytes=40 * 2**20),
+    )(adjoint, legendre)
 
 
 def make_basis(wave_numbers, lon_count, wave_total):
@@ -16,7 +364,7 @@
     return jnp.stack([factor * jnp.cos(angles), -factor * jnp.sin(angles)]).astype(jnp.bfloat16)
 
 
-def on_device(
+def in_general(
     probes_spec, legendre, wave_order, obs_weight, send_rows, send_counts, interp_idx, interp_weight
 ):
     band_count = lax.axis_size("band")
@@ -93,6 +441,13 @@
     return result.reshape(item_count, field_count, 2, slot_local, degree_count).astype(jnp.bfloat16)
 
 
+def on_device(probes_spec, legendre, wave_order, obs_weight, send_rows, *others):
+    sizes = lax.axis_size("band"), lax.axis_size("wave")
+    fits = fits_kernels(probes_spec, legendre, wave_order, obs_weight, send_rows, *sizes)
+    run = in_kernels if fits else in_general
+    return run(probes_spec, legendre, wave_order, obs_weight, send_rows, *others)
+
+
 def solution(mesh):
     placed = (
         P(("groups", "probe"), None, None, ("band", "wave"), None),

time: 309 us -> 35.5 us (0.11)
  other arithmetic: 133 us -> 0 us
  matrix products: 86.1 us -> 0 us
  local copies, waits for them, and re-layouts: 48.3 us -> 6.11 us
  Pallas kernels: 0 us -> 28.9 us
  starting transfers between devices: 16.6 us -> 0 us
  waiting for transfers between devices: 11.5 us -> 0 us
  blocking collectives: 9.94 us -> 0 us
    scatter-add x1 -> x0, other arithmetic: 103 us -> none  [on_device(): adjoint = jnp.zeros((probe_local, field_local, points), jnp.float32).at[:...]
    dot_general x4 -> x0, matrix products: 86.1 us -> none  [the longest x1 66.7 us: on_device(): jnp.einsum('pwgksn,sbln->bwpglks', spec_split, legendre_split, preferred_...]
    pallas_call x0 -> x2, Pallas kernels: none -> 28.9 us  [the longest x1 23.6 us: in_kernels(): pl.pallas_call(functools.partial(exchange_kernel, bands, waves), out_shap...]
    all_to_all x3 -> x0, starting transfers between devices: 16.6 us -> none  [the longest x1 7.25 us: on_device(): lax.all_to_all(flat_fourier, ('band', 'wave'), split_axis=0, concat_axis=...]
    convert_element_type x4 -> x0, local copies, waits for them, and re-layouts: 16 us -> none  [the longest x1 9.27 us: on_device(): result.reshape(item_count, field_count, 2, slot_local, degree_count)]
    another operation x1 -> x0, other arithmetic: 15.9 us -> none
    reshape x6 -> x1, local copies, waits for them, and re-layouts: 16.4 us -> 0.69 us  [in_kernels(): wave_order.reshape(1, total)]
    all_to_all x3 -> x0, waiting for transfers between devices: 11.5 us -> none  [the longest x1 6.25 us: on_device(): lax.all_to_all(scaled, ('band', 'wave'), split_axis=2, concat_axis=2, til...]
  transfers between devices with their start and end apart: 3 -> 0, of which waited for: 2 -> 0; matrix products, arithmetic and copies ran while one was open for 7% -> 0% of each run, Pallas kernels for 0% -> 0%
where the time goes in v1:
time: 35.5 us; the launch traced here: 35 us
  Pallas kernels  28.9 us (81%)
  local copies, waits for them, and re-layouts  6.11 us (17%)
    pallas_call x1, Pallas kernels, in_kernels(): pl.pallas_call(functools.partial(exchange_kernel, bands, waves), out_shap...  23.6 us
    unnamed x12, local copies, waits for them, and re-layouts  5.42 us
    pallas_call x1, Pallas kernels, in_kernels(): pl.pallas_call(synthesis_kernel, grid=(blocks,), out_shape=jax.ShapeDtype...  5.29 us

profile of v1, /device:TPU:0, one launch (start us, length us, event | category | flops | bytes accessed | tf_op | source)
XLA Modules:
  0.0 35.0 jit_solution(14006795902906695165)
XLA Ops:
  0.0 0.7 %reshape.3.wave_ref = s32[1,640]{1,0:T(1,128)S(1)} reshape(s32[640]{0:T(1024)} %param.10) | data formatting | bytes 5120 | tf_op jit(solution)/shard_map/reshape | solution.py:340
  0.7 0.0 copy-start
  0.7 1.9 %copy-done = bf16[80,16,1280]{2,1,0:T(8,128)(2,1)S(1)} copy-done((bf16[80,16,1280]{2,1,0:T(8,128)(2,1)S(1)}, bf16[80,16,1280]{2,1,0:T(8,128)(2,1)}, u32[]{:S(2)}) %copy-start) | copy-done | bytes 3276824
  2.6 0.0 copy-start.1
  2.6 0.7 %copy-done.1 = s32[4,1,8,32]{3,2,1,0:T(8,128)S(1)} copy-done((s32[4,1,8,32]{3,2,1,0:T(8,128)S(1)}, s32[4,1,8,32]{3,2,1,0:T(8,128)}, u32[]{:S(2)}) %copy-start.1) | copy-done | bytes 4120
  3.3 0.0 copy-start.2
  3.3 0.7 %copy-done.2 = f32[4,1,8,32]{3,2,1,0:T(8,128)S(1)} copy-done((f32[4,1,8,32]{3,2,1,0:T(8,128)S(1)}, f32[4,1,8,32]{3,2,1,0:T(8,128)}, u32[]{:S(2)}) %copy-start.2) | copy-done | bytes 4120
  4.1 0.0 copy-start.3
  4.1 0.7 %copy-done.3 = f32[4,256]{1,0:T(4,128)S(1)} copy-done((f32[4,256]{1,0:T(4,128)S(1)}, f32[4,256]{1,0:T(4,128)}, u32[]{:S(2)}) %copy-start.3) | copy-done | bytes 4120
  4.7 0.0 copy-start.4
  4.7 0.7 %copy-done.4 = s32[1,8,32]{2,1,0:T(8,128)S(1)} copy-done((s32[1,8,32]{2,1,0:T(8,128)S(1)}, s32[1,8,32]{2,1,0:T(8,128)}, u32[]{:S(2)}) %copy-start.4) | copy-done | bytes 1048
  5.4 0.0 copy-start.5
  5.4 0.7 %copy-done.5 = s32[8,8]{1,0:T(8,128)S(1)} copy-done((s32[8,8]{1,0:T(8,128)S(1)}, s32[8,8]{1,0:T(8,128)}, u32[]{:S(2)}) %copy-start.5) | copy-done | bytes 280
  6.1 23.6 %shard_map.82.adjoint_ref = bf16[2,128,160]{2,1,0:T(8,128)(2,1)S(1)} custom-call(bf16[2,8,2,80,1280]{4,3,2,1,0:T(8,128)(2,1)} %probes_hbm.1, bf16[80,16,1280]{2,1,0:T(8,128)(2,1)S(1)} %copy-done, s32[1,640]{1,0:T(1,128)S(1)} %reshape.3.wave_ref, f32[4,256]{1,0:T(4,128)S(1)} %copy-done.3, s32[1,8,32]{2,1,0:T(8,128)S(1)} %copy-done.4, s32[8,8]{1,0:T(8,128)S(1)} %copy-done.5, ...), custom_call_target="tpu_custom_call" | custom-call | tf_op jit(solution)/shard_map/pallas_call | solution.py:306
  29.8 5.3 %shard_map.83 = bf16[2,8,2,80,1280]{4,3,2,1,0:T(8,128)(2,1)} custom-call(bf16[2,128,160]{2,1,0:T(8,128)(2,1)S(1)} %shard_map.82.adjoint_ref, bf16[80,16,1280]{2,1,0:T(8,128)(2,1)S(1)} %copy-done), custom_call_target="tpu_custom_call" | custom-call | tf_op jit(solution)/shard_map/pallas_call | solution.py:343
Async XLA Ops:
  0.7 1.9 %copy-start = (bf16[80,16,1280]{2,1,0:T(8,128)(2,1)S(1)}, bf16[80,16,1280]{2,1,0:T(8,128)(2,1)}, u32[]{:S(2)}) copy-start(bf16[80,16,1280]{2,1,0:T(8,128)(2,1)} %legendre_ref.1) | copy-start | bytes 9830404
  2.6 0.7 %copy-start.1 = (s32[4,1,8,32]{3,2,1,0:T(8,128)S(1)}, s32[4,1,8,32]{3,2,1,0:T(8,128)}, u32[]{:S(2)}) copy-start(s32[4,1,8,32]{3,2,1,0:T(8,128)} %idx_ref.1) | copy-start | bytes 12292
  3.3 0.7 %copy-start.2 = (f32[4,1,8,32]{3,2,1,0:T(8,128)S(1)}, f32[4,1,8,32]{3,2,1,0:T(8,128)}, u32[]{:S(2)}) copy-start(f32[4,1,8,32]{3,2,1,0:T(8,128)} %weight_ref.1) | copy-start | bytes 12292
  4.1 0.7 %copy-start.3 = (f32[4,256]{1,0:T(4,128)S(1)}, f32[4,256]{1,0:T(4,128)}, u32[]{:S(2)}) copy-start(f32[4,256]{1,0:T(4,128)} %obs_ref.1) | copy-start | bytes 12292
  4.7 0.7 %copy-start.4 = (s32[1,8,32]{2,1,0:T(8,128)S(1)}, s32[1,8,32]{2,1,0:T(8,128)}, u32[]{:S(2)}) copy-start(s32[1,8,32]{2,1,0:T(8,128)} %rows_ref.1) | copy-start | bytes 3076
  5.4 0.7 %copy-start.5 = (s32[8,8]{1,0:T(8,128)S(1)}, s32[8,8]{1,0:T(8,128)}, u32[]{:S(2)}) copy-start(s32[8,8]{1,0:T(8,128)} %counts_ref.1) | copy-start | bytes 772

commit v2 on v1

--- a/solution.py
+++ b/solution.py
@@ -40,14 +40,15 @@
 def selector(lat, items):
     shape = (lat * items, items * SB * lat)
     row, col = iota(shape, 0), iota(shape, 1)
-    same = (row // items == col % lat) & (row % items == col // (SB * lat))
+    item_bits, span_bits = items.bit_length() - 1, (SB * lat).bit_length() - 1
+    same = (row >> item_bits == col & lat - 1) & (row & items - 1 == col >> span_bits)
     return jnp.where(same, 1.0, 0.0).astype(BF16)
 
 
 def exchange_kernel(
-    bands, waves, probes_hbm, legendre_hbm, wave_ref, obs_ref, rows_ref, counts_ref, idx_ref,
-    weight_ref, out_ref, probe_buf, leg_buf, spread, basis, corner, send_w, recv_w, slot_w,
-    send_1, recv_1, send_2, recv_2, lanes, point, weights, probe_sem, leg_sem, tx_w, rx_w, tx_1,
+    bands, waves, probes_hbm, legendre_hbm, wave_hbm, obs_hbm, rows_hbm, counts_hbm, idx_hbm,
+    weight_hbm, out_ref, wave_ref, obs_ref, rows_ref, counts_ref, idx_ref, weight_ref, probe_buf, leg_buf, spread, basis, corner, send_w, recv_w, slot_w,
+    send_1, recv_1, send_2, recv_2, lanes, point, weights, small_sem, probe_sem, leg_sem, tx_w, rx_w, tx_1,
     rx_1, tx_2, rx_2,
 ):
     nodes = bands * waves
@@ -91,14 +92,62 @@
             pltpu.make_async_copy(legendre_hbm.at[part], leg_buf.at[block], leg_sem.at[block]),
         )
 
+    smalls = [
+        pltpu.make_async_copy(source, target, small_sem.at[i])
+        for i, (source, target) in enumerate(
+            (
+                (obs_hbm, obs_ref),
+                (rows_hbm, rows_ref),
+                (counts_hbm, counts_ref),
+                (idx_hbm, idx_ref),
+                (weight_hbm, weight_ref),
+                (wave_hbm, wave_ref),
+            )
+        )
+    ]
     for block in range(blocks):
         for one in load(block):
             one.start()
+    for one in smalls:
+        one.start()
     barrier = pltpu.get_barrier_semaphore()
     for step in range(1, nodes):
         pl.semaphore_signal(
             barrier, inc=1, device_id=where_is(peer(step)), device_id_type=pl.DeviceIdType.MESH
         )
+
+    choose = selector(lat, items)
+    @pl.loop(0, blocks)
+    def _(block):
+        for one in load(block):
+            one.wait()
+        product = dot(
+            probe_buf[block].reshape(probe_local * field_count * 2 * SB, degrees),
+            leg_buf[block].reshape(SB * lat, degrees),
+            NT,
+        )
+        own = iota(product.shape, 0) & SB - 1 == iota(product.shape, 1) >> lat.bit_length() - 1
+        product = jnp.where(own, product, 0.0).astype(BF16)
+        for p in range(probe_local):
+            for w in range(waves):
+                for e in range(fields):
+                    for k in range(2):
+                        first = (((p * waves + w) * fields + e) * 2 + k) * SB
+                        item = (p * fields + e) * SB * lat
+                        spread[w, k, block, :, item : item + SB * lat] = product[first : first + SB]
+
+    for w in range(waves):
+        fourier = dot(choose, spread[w].reshape(2 * slots, items * SB * lat), NT).astype(BF16)
+        for b in range(bands):
+            send_1[b * waves + w] = fourier[b * rows : (b + 1) * rows]
+    pl.semaphore_wait(barrier, nodes - 1)
+    copies_1 = copies(send_1, recv_1, tx_1, rx_1)
+    for one in copies_1:
+        one.start()
+    recv_1[me] = send_1[me]
+
+    for one in smalls:
+        one.wait()
 
     obs = jnp.concatenate([obs_ref[...]] * probe_local, axis=0)
     high = obs.astype(BF16).astype(F32)
@@ -109,7 +158,6 @@
         pick = iota((obs.shape[1], capacity), 0) == record[node : node + 1, :]
         found = dot(split, jnp.where(pick, 1.0, 0.0).astype(BF16))
         send_w[node] = found[2 * items :] + found[items : 2 * items] + found[:items]
-    pl.semaphore_wait(barrier, nodes - 1)
     copies_w = copies(send_w, recv_w, tx_w, rx_w)
     for one in copies_w:
         one.start()
@@ -128,39 +176,9 @@
             at = slice(node * capacity, (node + 1) * capacity)
             point[i : i + 1, at] = idx_ref[i, 0, node : node + 1, :].astype(F32)
 
-    choose = selector(lat, items)
-
-    @pl.loop(0, blocks)
-    def _(block):
-        for one in load(block):
-            one.wait()
-        product = dot(
-            probe_buf[block].reshape(probe_local * field_count * 2 * SB, degrees),
-            leg_buf[block].reshape(SB * lat, degrees),
-            NT,
-        )
-        own = iota(product.shape, 0) % SB == iota(product.shape, 1) // lat
-        product = jnp.where(own, product, 0.0).astype(BF16)
-        for p in range(probe_local):
-            for w in range(waves):
-                for e in range(fields):
-                    for k in range(2):
-                        first = (((p * waves + w) * fields + e) * 2 + k) * SB
-                        item = (p * fields + e) * SB * lat
-                        spread[w, k, block, :, item : item + SB * lat] = product[first : first + SB]
-
-    for w in range(waves):
-        fourier = dot(choose, spread[w].reshape(2 * slots, items * SB * lat), NT).astype(BF16)
-        for b in range(bands):
-            send_1[b * waves + w] = fourier[b * rows : (b + 1) * rows]
-    copies_1 = copies(send_1, recv_1, tx_1, rx_1)
-    for one in copies_1:
-        one.start()
-    recv_1[me] = send_1[me]
-
     factor = 1.0 / math.sqrt(total)
     for lane in range(0, total, 128):
-        order = wave_ref[:, lane : lane + 128].astype(F32)
+        order = wave_ref[lane : lane + 128].reshape(1, 128).astype(F32)
         turn_c, turn_s = cos_sin(order * 128.0)
 
         @pl.loop(0, 2)
@@ -250,7 +268,8 @@
         choose = selector(lat, items)
         for w in range(waves):
             wide = dot(adjoint_ref[w], choose, TN)
-            own = iota(wide.shape, 0) % SB == iota(wide.shape, 1) % (SB * lat) // lat
+            column = iota(wide.shape, 1) & SB * lat - 1
+            own = iota(wide.shape, 0) & SB - 1 == column >> lat.bit_length() - 1
             spread[w] = jnp.where(own, wide, 0.0).astype(BF16).reshape(spread.shape[1:])
 
     pieces = []
@@ -301,14 +320,20 @@
     capacity = send_rows.shape[2]
     wide = items * SB * lat
     vmem = pl.BlockSpec(memory_space=pltpu.VMEM)
-    hbm = pl.BlockSpec(memory_space=pl.ANY)
+    hbm = pl.BlockSpec(memory_space=pltpu.HBM)
     dma = pltpu.SemaphoreType.DMA
     adjoint = pl.pallas_call(
         functools.partial(exchange_kernel, bands, waves),
         out_shape=jax.ShapeDtypeStruct((waves, bands * rows, 2 * slots), BF16),
-        in_specs=[hbm, hbm] + [vmem] * 6,
+        in_specs=[hbm] * 8,
         out_specs=vmem,
         scratch_shapes=[
+            pltpu.VMEM(wave_order.shape, jnp.int32),
+            pltpu.VMEM(obs_weight.shape, F32),
+            pltpu.VMEM(send_rows.shape, jnp.int32),
+            pltpu.VMEM(send_counts.shape, jnp.int32),
+            pltpu.VMEM(interp_idx.shape, jnp.int32),
+            pltpu.VMEM(interp_weight.shape, F32),
             pltpu.VMEM((blocks, probe_local, field_count, 2, SB, degrees), BF16),
             pltpu.VMEM((blocks, SB, lat, degrees), BF16),
             pltpu.VMEM((waves, 2, blocks, SB, wide), BF16),
@@ -324,6 +349,7 @@
             pltpu.VMEM((rows, 2 * total), F32),
             pltpu.VMEM((8, nodes * capacity), F32),
             pltpu.VMEM((8, nodes * capacity), F32),
+            dma((6,)),
             dma((blocks,)),
             dma((blocks,)),
             dma((nodes,)),
@@ -334,10 +360,10 @@
             dma((nodes,)),
         ],
         compiler_params=pltpu.CompilerParams(
-            collective_id=0, has_side_effects=True, vmem_limit_bytes=48 * 2**20
+            collective_id=0, has_side_effects=True, vmem_limit_bytes=64 * 2**20
         ),
     )(
-        probes_spec, legendre, wave_order.reshape(1, total), obs_weight, send_rows, send_counts,
+        probes_spec, legendre, wave_order, obs_weight, send_rows, send_counts,
         interp_idx, interp_weight,
     )
     return pl.pallas_call(
@@ -352,7 +378,7 @@
             (probe_local, field_count, 2, SB, degrees), lambda i: (0, 0, 0, i, 0)
         ),
         scratch_shapes=[pltpu.VMEM((waves, 2, blocks, SB, wide), BF16)],
-        compiler_params=pltpu.CompilerParams(vmem_limit_bytes=40 * 2**20),
+        compiler_params=pltpu.CompilerParams(vmem_limit_bytes=64 * 2**20),
     )(adjoint, legendre)
 
 

time: 35.5 us -> 29.7 us (0.84)
  local copies, waits for them, and re-layouts: 6.11 us -> 0 us
  Pallas kernels: 28.9 us -> 29.4 us
    unnamed x12 -> x0, local copies, waits for them, and re-layouts: 5.42 us -> none
    pallas_call x1, Pallas kernels: 5.29 us -> 7.48 us  [in_kernels(): pl.pallas_call(synthesis_kernel, grid=(blocks,), out_shape=jax.ShapeDtype...]
    pallas_call x1, Pallas kernels: 23.6 us -> 22 us  [in_kernels(): pl.pallas_call(functools.partial(exchange_kernel, bands, waves), out_shap...]
    reshape x1 -> x0, local copies, waits for them, and re-layouts: 0.69 us -> none  [in_kernels(): wave_order.reshape(1, total)]
where the time goes in v2:
time: 29.7 us; the launch traced here: 29.4 us
  Pallas kernels  29.4 us (99%)
    pallas_call x1, Pallas kernels, in_kernels(): pl.pallas_call(functools.partial(exchange_kernel, bands, waves), out_shap...  22 us
    pallas_call x1, Pallas kernels, in_kernels(): pl.pallas_call(synthesis_kernel, grid=(blocks,), out_shape=jax.ShapeDtype...  7.48 us

profile of v2, /device:TPU:0, one launch (start us, length us, event | category | flops | bytes accessed | tf_op | source)
XLA Modules:
  0.0 29.4 jit_solution(18389117772689754390)
XLA Ops:
  0.0 22.0 %shard_map.82.adjoint_ref = bf16[2,128,160]{2,1,0:T(8,128)(2,1)} custom-call(bf16[2,8,2,80,1280]{4,3,2,1,0:T(8,128)(2,1)} %probes_hbm.1, bf16[80,16,1280]{2,1,0:T(8,128)(2,1)} %legendre_ref.1, s32[640]{0:T(1024)} %wave_hbm.1, f32[4,256]{1,0:T(4,128)} %obs_hbm.1, s32[1,8,32]{2,1,0:T(8,128)} %rows_hbm.1, s32[8,8]{1,0:T(8,128)} %counts_hbm.1, ...), custom_call_target="tpu_custom_call" | custom-call | tf_op jit(solution)/shard_map/pallas_call | solution.py:325
  22.0 7.5 %shard_map.83 = bf16[2,8,2,80,1280]{4,3,2,1,0:T(8,128)(2,1)} custom-call(bf16[2,128,160]{2,1,0:T(8,128)(2,1)} %shard_map.82.adjoint_ref, bf16[80,16,1280]{2,1,0:T(8,128)(2,1)} %legendre_ref.1), custom_call_target="tpu_custom_call" | custom-call | tf_op jit(solution)/shard_map/pallas_call | solution.py:369

commit v3 on v2

--- a/solution.py
+++ b/solution.py
@@ -360,11 +360,16 @@
             dma((nodes,)),
         ],
         compiler_params=pltpu.CompilerParams(
-            collective_id=0, has_side_effects=True, vmem_limit_bytes=64 * 2**20
+            collective_id=0, has_side_effects=True, vmem_limit_bytes=40 * 2**20
         ),
     )(
-        probes_spec, legendre, wave_order, obs_weight, send_rows, send_counts,
-        interp_idx, interp_weight,
+        *(
+            pltpu.with_memory_space_constraint(one, pltpu.HBM)
+            for one in (
+                probes_spec, legendre, wave_order, obs_weight, send_rows, send_counts, interp_idx,
+                interp_weight,
+            )
+        )
     )
     return pl.pallas_call(
         synthesis_kernel,
@@ -378,7 +383,7 @@
             (probe_local, field_count, 2, SB, degrees), lambda i: (0, 0, 0, i, 0)
         ),
         scratch_shapes=[pltpu.VMEM((waves, 2, blocks, SB, wide), BF16)],
-        compiler_params=pltpu.CompilerParams(vmem_limit_bytes=64 * 2**20),
+        compiler_params=pltpu.CompilerParams(vmem_limit_bytes=40 * 2**20),
     )(adjoint, legendre)
 
 

time: 29.7 us -> 26.9 us (0.906)
  Pallas kernels: 29.4 us -> 26.8 us
    pallas_call x1, Pallas kernels: 7.48 us -> 5.29 us  [in_kernels(): pl.pallas_call(synthesis_kernel, grid=(blocks,), out_shape=jax.ShapeDtype...]
    pallas_call x1, Pallas kernels: 22 us -> 21.5 us  [in_kernels(): pl.pallas_call(functools.partial(exchange_kernel, bands, waves), out_shap...]
where the time goes in v3:
time: 26.9 us; the launch traced here: 26.8 us
  Pallas kernels  26.8 us (100%)
    pallas_call x1, Pallas kernels, in_kernels(): pl.pallas_call(functools.partial(exchange_kernel, bands, waves), out_shap...  21.5 us
    pallas_call x1, Pallas kernels, in_kernels(): pl.pallas_call(synthesis_kernel, grid=(blocks,), out_shape=jax.ShapeDtype...  5.29 us

profile of v3, /device:TPU:0, one launch (start us, length us, event | category | flops | bytes accessed | tf_op | source)
XLA Modules:
  0.0 26.8 jit_solution(16094002363753944190)
XLA Ops:
  0.0 0.0 copy-start
  0.0 21.5 %shard_map.82.adjoint_ref = bf16[2,128,160]{2,1,0:T(8,128)(2,1)S(1)} custom-call(bf16[2,8,2,80,1280]{4,3,2,1,0:T(8,128)(2,1)} %probes_hbm.1, bf16[80,16,1280]{2,1,0:T(8,128)(2,1)} %legendre_ref.1, s32[640]{0:T(1024)} %wave_hbm.1, f32[4,256]{1,0:T(4,128)} %obs_hbm.1, s32[1,8,32]{2,1,0:T(8,128)} %rows_hbm.1, s32[8,8]{1,0:T(8,128)} %counts_hbm.1, ...), custom_call_target="tpu_custom_call" | custom-call | tf_op jit(solution)/shard_map/pallas_call | solution.py:325
  21.5 0.0 copy-done
  21.5 5.3 %shard_map.83 = bf16[2,8,2,80,1280]{4,3,2,1,0:T(8,128)(2,1)} custom-call(bf16[2,128,160]{2,1,0:T(8,128)(2,1)S(1)} %shard_map.82.adjoint_ref, bf16[80,16,1280]{2,1,0:T(8,128)(2,1)S(1)} %copy-done), custom_call_target="tpu_custom_call" | custom-call | tf_op jit(solution)/shard_map/pallas_call | solution.py:374
Async XLA Ops:
  0.0 21.5 %copy-start = (bf16[80,16,1280]{2,1,0:T(8,128)(2,1)S(1)}, bf16[80,16,1280]{2,1,0:T(8,128)(2,1)}, u32[]{:S(2)}) copy-start(bf16[80,16,1280]{2,1,0:T(8,128)(2,1)} %legendre_ref.1) | copy-start | bytes 9830404

commit v4 on v3

--- a/solution.py
+++ b/solution.py
@@ -43,6 +43,11 @@
     item_bits, span_bits = items.bit_length() - 1, (SB * lat).bit_length() - 1
     same = (row >> item_bits == col & lat - 1) & (row & items - 1 == col >> span_bits)
     return jnp.where(same, 1.0, 0.0).astype(BF16)
+
+
+def own_slot(lat):
+    shape = (SB, SB * lat)
+    return iota(shape, 0) == iota(shape, 1) >> lat.bit_length() - 1
 
 
 def exchange_kernel(
@@ -126,15 +131,15 @@
             leg_buf[block].reshape(SB * lat, degrees),
             NT,
         )
-        own = iota(product.shape, 0) & SB - 1 == iota(product.shape, 1) >> lat.bit_length() - 1
-        product = jnp.where(own, product, 0.0).astype(BF16)
+        own = own_slot(lat)
         for p in range(probe_local):
             for w in range(waves):
                 for e in range(fields):
                     for k in range(2):
                         first = (((p * waves + w) * fields + e) * 2 + k) * SB
                         item = (p * fields + e) * SB * lat
-                        spread[w, k, block, :, item : item + SB * lat] = product[first : first + SB]
+                        piece = jnp.where(own, product[first : first + SB], 0.0)
+                        spread[w, k, block, :, item : item + SB * lat] = piece.astype(BF16)
 
     for w in range(waves):
         fourier = dot(choose, spread[w].reshape(2 * slots, items * SB * lat), NT).astype(BF16)
@@ -214,10 +219,6 @@
                 at_west, west_weight[l], jnp.where(at_east, east_weight[l], 0.0)
             ).astype(BF16)
 
-    for one in copies_w:
-        one.wait()
-    for node in range(nodes):
-        slot_w[:, node * capacity : (node + 1) * capacity] = recv_w[node]
     for one in copies_1:
         one.wait()
     for node in range(nodes):
@@ -233,6 +234,10 @@
         both = jnp.concatenate([here, here - here.astype(BF16).astype(F32)], axis=0)
         observed += dot(both.astype(BF16), corner[l].reshape(NLON, nodes * capacity))
     observed = (observed[:items] + observed[items:]).astype(BF16).astype(F32)
+    for one in copies_w:
+        one.wait()
+    for node in range(nodes):
+        slot_w[:, node * capacity : (node + 1) * capacity] = recv_w[node]
     weighted = (slot_w[...] * observed).astype(BF16)
     adjoint = jnp.concatenate(
         [dot(weighted, corner[l].reshape(NLON, nodes * capacity), NT) for l in range(lat_local)],
@@ -268,17 +273,16 @@
         choose = selector(lat, items)
         for w in range(waves):
             wide = dot(adjoint_ref[w], choose, TN)
-            column = iota(wide.shape, 1) & SB * lat - 1
-            own = iota(wide.shape, 0) & SB - 1 == column >> lat.bit_length() - 1
-            spread[w] = jnp.where(own, wide, 0.0).astype(BF16).reshape(spread.shape[1:])
-
+            spread[w] = wide.astype(BF16).reshape(spread.shape[1:])
+
+    own = jnp.where(own_slot(lat), 1.0, 0.0).astype(BF16)
     pieces = []
     for p in range(probe_local):
         for w in range(waves):
             for e in range(fields):
                 for k in range(2):
                     item = (p * fields + e) * SB * lat
-                    pieces.append(spread[w, k, block, :, item : item + SB * lat])
+                    pieces.append(own * spread[w, k, block, :, item : item + SB * lat])
     result = dot(
         jnp.concatenate(pieces, axis=0), legendre_ref[...].reshape(SB * lat, degrees)
     )

time: 26.9 us -> 26.6 us (0.989)
  Pallas kernels: 26.8 us -> 26.5 us
    pallas_call x1, Pallas kernels: 21.5 us -> 21.2 us  [in_kernels(): pl.pallas_call(functools.partial(exchange_kernel, bands, waves), out_shap...]
where the time goes in v4:
time: 26.6 us; the launch traced here: 26.5 us
  Pallas kernels  26.5 us (100%)
    pallas_call x1, Pallas kernels, in_kernels(): pl.pallas_call(functools.partial(exchange_kernel, bands, waves), out_shap...  21.2 us
    pallas_call x1, Pallas kernels, in_kernels(): pl.pallas_call(synthesis_kernel, grid=(blocks,), out_shape=jax.ShapeDtype...  5.29 us

profile of v4, /device:TPU:0, one launch (start us, length us, event | category | flops | bytes accessed | tf_op | source)
XLA Modules:
  0.0 26.5 jit_solution(15560679295399792780)
XLA Ops:
  0.0 0.0 copy-start
  0.0 21.2 %shard_map.82.adjoint_ref = bf16[2,128,160]{2,1,0:T(8,128)(2,1)S(1)} custom-call(bf16[2,8,2,80,1280]{4,3,2,1,0:T(8,128)(2,1)} %probes_hbm.1, bf16[80,16,1280]{2,1,0:T(8,128)(2,1)} %legendre_ref.1, s32[640]{0:T(1024)} %wave_hbm.1, f32[4,256]{1,0:T(4,128)} %obs_hbm.1, s32[1,8,32]{2,1,0:T(8,128)} %rows_hbm.1, s32[8,8]{1,0:T(8,128)} %counts_hbm.1, ...), custom_call_target="tpu_custom_call" | custom-call | tf_op jit(solution)/shard_map/pallas_call | solution.py:329
  21.2 0.0 copy-done
  21.2 5.3 %shard_map.83 = bf16[2,8,2,80,1280]{4,3,2,1,0:T(8,128)(2,1)} custom-call(bf16[2,128,160]{2,1,0:T(8,128)(2,1)S(1)} %shard_map.82.adjoint_ref, bf16[80,16,1280]{2,1,0:T(8,128)(2,1)S(1)} %copy-done), custom_call_target="tpu_custom_call" | custom-call | tf_op jit(solution)/shard_map/pallas_call | solution.py:378
Async XLA Ops:
  0.0 21.2 %copy-start = (bf16[80,16,1280]{2,1,0:T(8,128)(2,1)S(1)}, bf16[80,16,1280]{2,1,0:T(8,128)(2,1)}, u32[]{:S(2)}) copy-start(bf16[80,16,1280]{2,1,0:T(8,128)(2,1)} %legendre_ref.1) | copy-start | bytes 9830404
